TPU v7x, 32 devices: a whole 2x2x4 slice. The times are simulated.
32 devices in a mesh: shift: 4 (over y, x), rows: 8 (over z, core).
Axes of the slice: x: 2, y: 2, z: 4, core: 2. Of those that a mesh axis runs over, the one named last changes fastest.
Arguments:
- zc_in: bfloat16 [4, 512, 16384], P('shift', 'rows'), may hold values from -6 to 6
- zo_in: bfloat16 [4, 384, 16384], P('shift', 'rows'), may hold values from -6 to 6
- count_c: int32 [4], replicated, may hold values from 256 to 512, as said below
- count_o: int32 [4], replicated, may hold values from 192 to 384, as said below
- mass: bfloat16 [128, 4, 128, 128], P(('shift', 'rows')), may hold values from -0.25 to 0.25
- adjacency: int32 [128, 4], P(('shift', 'rows')), may hold values from 0 to 127, as said below
- ghost_len: int32 [128, 4], P(('shift', 'rows')), may hold values from 1 to 128, as said below
- omega: float32 [2048, 128], replicated, may hold values from -6 to 6
Outputs:
- proj_c: float32 [128, 16384], P(None, ('shift', 'rows'))
- proj_o: float32 [128, 16384], P(None, ('shift', 'rows'))
Inputs may be any that keep to these rules, and one draw needn't show every extreme that they name: `count_c`: each entry is 256 or more, and one group holds 512 exactly. `count_o`: each entry is 192 or more, and one group holds 384 exactly. adjacency[i, 0] = i, and every entry lies within 2 blocks of i. ghost_len[i, 0] = 128.
All inputs are finite; a program needn't handle non-finite values.
Results may differ from a plain program's by a relative error of at most 0.0047.
Values may be sent and summed in bfloat16 or wider, within the bound.
A program may use at most 128 MiB of HBM per device.

v0:
```python
import jax
import jax.numpy as jnp
from jax import lax
from jax.sharding import PartitionSpec as P

REACH = 2
AXES = ("shift", "rows")
F32 = jnp.float32
BF16 = jnp.bfloat16


def split(matrix):
    high = lax.reduce_precision(matrix, 8, 7)
    return jnp.concatenate([high.astype(BF16), (matrix - high).astype(BF16)], axis=-1)


def joined(matrix):
    half = matrix.shape[-1] // 2
    return matrix[..., :half] + matrix[..., half:]


def dot(left, right, contract_left, contract_right):
    return lax.dot_general(
        left, right, (((contract_left,), (contract_right,)), ((), ())), preferred_element_type=F32
    )


def live(counts, slots):
    inner = jnp.arange(slots, dtype=jnp.int32)
    return (inner[None, :] < counts[:, None]).reshape(-1, 1)


def orth_local(matrix):
    square = jnp.dot(matrix.T, matrix, precision=lax.Precision.HIGHEST)
    lower = jnp.linalg.cholesky(square)
    return jax.scipy.linalg.solve_triangular(lower, matrix.T, lower=True).T


def per_device(zc_in, zo_in, count_c, count_o, mass, adjacency, ghost_len, omega):
    index = lax.axis_index(AXES)
    devices = lax.axis_size(AXES)
    zc = lax.all_to_all(zc_in[0], AXES, split_axis=1, concat_axis=0, tiled=True)
    zo = lax.all_to_all(zo_in[0], AXES, split_axis=1, concat_axis=0, tiled=True)
    groups = count_c.shape[0]
    live_c = live(count_c, zc.shape[0] // groups)
    live_o = live(count_o, zo.shape[0] // groups)
    size = mass.shape[2]
    count, near = adjacency.shape
    local = adjacency - index * count + REACH
    inner = jnp.arange(size, dtype=jnp.int32)
    masked = jnp.where(inner < ghost_len[:, :, None, None], mass, jnp.zeros_like(mass))
    places = jnp.arange(count + 2 * REACH, dtype=jnp.int32)
    hit = (local[:, :, None] == places)[:, :, None, :, None]
    dense = jnp.where(hit, masked[:, :, :, None, :].astype(F32), 0.0).sum(axis=1)
    dense = dense.reshape(count * size, -1)
    banded = lax.reduce_precision(dense, 8, 7)
    banded_rest = (dense - banded).astype(BF16)
    banded = banded.astype(BF16)
    up = [(i, i + 1) for i in range(devices - 1)]
    down = [(j, i) for i, j in up]
    edge = REACH * size
    width = omega.shape[1]

    def forward(right):
        rows = joined(dot(zc, split(right), 0, 0))
        before = lax.ppermute(rows[-edge:], AXES, up)
        after = lax.ppermute(rows[:edge], AXES, down)
        wide = split(jnp.concatenate([before, rows, after], axis=0))
        mixed = joined(dot(banded, wide, 1, 0) + dot(banded_rest, wide, 1, 0))
        part = joined(dot(zo, split(mixed), 1, 0))
        return jnp.where(live_o, lax.psum(part, AXES), 0.0)

    def backward(left):
        rows = dot(zo, split(left), 0, 0)
        rows = split(joined(rows))
        wide = joined(dot(banded, rows, 0, 0) + dot(banded_rest, rows, 0, 0))
        above = lax.ppermute(wide[-edge:], AXES, up)
        below = lax.ppermute(wide[:edge], AXES, down)
        rows = wide[edge:-edge]
        rows = rows + jnp.pad(above, ((0, rows.shape[0] - edge), (0, 0)))
        rows = rows + jnp.pad(below, ((rows.shape[0] - edge, 0), (0, 0)))
        part = joined(dot(zc, split(rows), 1, 0))
        return jnp.where(live_c, lax.psum(part, AXES), 0.0)

    first = orth_local(forward(jnp.where(live_c, omega, 0.0)))
    right = orth_local(backward(first))
    proj_c = dot(right.astype(BF16), zc, 0, 0)
    left = orth_local(forward(right))
    proj_o = dot(left.astype(BF16), zo, 0, 0)
    return (proj_c, proj_o)


def solution(mesh):
    placed = (
        P("shift", "rows", None),
        P("shift", "rows", None),
        P(),
        P(),
        P(AXES, None, None, None),
        P(AXES, None),
        P(AXES, None),
        P(),
    )
    return jax.shard_map(
        per_device,
        mesh=mesh,
        in_specs=placed,
        out_specs=(P(None, AXES), P(None, AXES)),
        check_vma=False,
    )
```

profile of v0, /device:TPU:0, one launch (start us, length us, event | category | flops | bytes accessed | tf_op | source)
XLA Modules:
  0.0 631.2 jit_solution(16880807980116318967)
XLA Ops:
  7.2 2.4 copy.38
  9.5 2.5 copy.31
  12.0 7.3 %all-to-all-start = ((bf16[64,32,512]{2,0,1:T(8,128)(2,1)}), bf16[64,32,512]{2,0,1:T(8,128)(2,1)S(1)}, u32[]{:S(2)}, u32[]{:S(2)}) async-start(bf16[64,32,512]{2,0,1:T(8,128)(2,1)} %copy.31), calls=%async_computation | async-start | bytes 4194304 | tf_op jit(solution)/shard_map/all_to_all | solution.py:42
  21.3 2.0 copy.32
  23.4 46.0 %all-to-all-done = bf16[64,32,512]{2,0,1:T(8,128)(2,1)S(1)} async-done(((bf16[64,32,512]{2,0,1:T(8,128)(2,1)}), bf16[64,32,512]{2,0,1:T(8,128)(2,1)S(1)}, u32[]{:S(2)}, u32[]{:S(2)}) %all-to-all-start) | async-done | bytes 2097184 | tf_op jit(solution)/shard_map/all_to_all | solution.py:42
  69.4 3.5 all-to-all-start.1
  81.0 2.2 collective-permute-done.1
  84.4 27.3 %all-to-all-done.1 = bf16[48,32,512]{2,0,1:T(8,128)(2,1)} async-done(((bf16[48,32,512]{2,0,1:T(8,128)(2,1)}), bf16[48,32,512]{2,0,1:T(8,128)(2,1)}, u32[]{:S(2)}, u32[]{:S(2)}) %all-to-all-start.1) | async-done | bytes 1572896 | tf_op jit(solution)/shard_map/all_to_all | solution.py:43
  111.8 2.0 convolution_bitcast_fusion.1
  115.4 129.2 %all-reduce.6.cloned.1.call-done = f32[1536,128]{0,1:T(8,128)} async-done(((f32[1536,128]{0,1:T(8,128)}), f32[1536,128]{0,1:T(8,128)}) %all-reduce.6.cloned.1.call-update) | async-done | bytes 786448 | tf_op jit(solution)/shard_map/psum | solution.py:71
  244.6 2.2 fusion.23
  247.0 11.7 %cholesky.59 = f32[128,128]{1,0:T(8,128)S(1)} custom-call(f32[128,128]{1,0:T(8,128)S(1)} %fusion.66), custom_call_target="Cholesky" | custom-call | tf_op jit(solution)/shard_map/jit(cholesky)/cholesky | solution.py:35
  260.0 9.8 %custom-call.11 = f32[1,128,128]{1,2,0:T(8,128)S(1)} custom-call(f32[1,128,128]{2,1,0:T(8,128)S(1)} %fusion.58), custom_call_target="InvertDiagBlocksLowerTriangular" | custom-call | tf_op jit(solution)/shard_map/jit(_solve_triangular)/triangular_solve | solution.py:36
  277.8 3.6 collective-permute-done.3
  283.5 136.5 %all-reduce.8.cloned.1.call-done = f32[2048,128]{0,1:T(8,128)} async-done(((f32[2048,128]{0,1:T(8,128)}), f32[2048,128]{0,1:T(8,128)}) %all-reduce.8.cloned.1.call-update) | async-done | bytes 1048592 | tf_op jit(solution)/shard_map/psum | solution.py:83
  420.0 2.7 fusion.11
  422.8 11.7 %cholesky.70 = f32[128,128]{1,0:T(8,128)S(1)} custom-call(f32[128,128]{1,0:T(8,128)S(1)} %fusion.64), custom_call_target="Cholesky" | custom-call | tf_op jit(solution)/shard_map/jit(cholesky)/cholesky | solution.py:35
  435.8 9.8 %custom-call.9 = f32[1,128,128]{1,2,0:T(8,128)S(1)} custom-call(f32[1,128,128]{2,1,0:T(8,128)S(1)} %fusion.59), custom_call_target="InvertDiagBlocksLowerTriangular" | custom-call | tf_op jit(solution)/shard_map/jit(_solve_triangular)/triangular_solve | solution.py:36
  451.2 3.4 collective-permute-done.5
  461.0 133.8 %all-reduce.10.cloned.1.call-done = f32[1536,128]{0,1:T(8,128)} async-done(((f32[1536,128]{0,1:T(8,128)}), f32[1536,128]{0,1:T(8,128)}) %all-reduce.10.cloned.1.call-update) | async-done | bytes 786448 | tf_op jit(solution)/shard_map/psum | solution.py:71
  594.8 2.2 fusion.20
  597.1 11.7 %cholesky.81 = f32[128,128]{1,0:T(8,128)S(1)} custom-call(f32[128,128]{1,0:T(8,128)S(1)} %fusion.62), custom_call_target="Cholesky" | custom-call | tf_op jit(solution)/shard_map/jit(cholesky)/cholesky | solution.py:35
  610.2 9.8 %custom-call.12 = f32[1,128,128]{1,2,0:T(8,128)S(1)} custom-call(f32[1,128,128]{2,1,0:T(8,128)S(1)} %fusion.60), custom_call_target="InvertDiagBlocksLowerTriangular" | custom-call | tf_op jit(solution)/shard_map/jit(_solve_triangular)/triangular_solve | solution.py:36
  622.0 2.5 fusion.92
  (92 shorter events, 40.9 us)
Async XLA Ops:
  12.0 57.4 %all-to-all-start = ((bf16[64,32,512]{2,0,1:T(8,128)(2,1)}), bf16[64,32,512]{2,0,1:T(8,128)(2,1)S(1)}, u32[]{:S(2)}, u32[]{:S(2)}) async-start(bf16[64,32,512]{2,0,1:T(8,128)(2,1)} %copy.31), calls=%async_computation | async-start | bytes 4194304 | tf_op jit(solution)/shard_map/all_to_all | solution.py:42
  21.3 2.0 copy-start.6
  23.3 49.7 %copy-start.8 = (s32[4]{0:T(128)S(1)}, s32[4]{0:T(128)}, u32[]{:S(2)}) copy-start(s32[4]{0:T(128)} %param.13) | copy-start | bytes 52
  23.4 51.2 %copy-start.7 = (s32[4,4]{1,0:T(4,128)S(1)}, s32[4,4]{1,0:T(4,128)}, u32[]{:S(2)}) copy-start(s32[4,4]{1,0:T(4,128)} %param.17) | copy-start | bytes 196
  69.4 6.6 %copy-start = (bf16[64,32,512]{2,0,1:T(8,128)(2,1)}, bf16[64,32,512]{2,0,1:T(8,128)(2,1)S(1)}, u32[]{:S(2)}) copy-start(bf16[64,32,512]{2,0,1:T(8,128)(2,1)S(1)} %all-to-all-done) | copy-start | bytes 6291460
  69.4 42.4 %all-to-all-start.1 = ((bf16[48,32,512]{2,0,1:T(8,128)(2,1)}), bf16[48,32,512]{2,0,1:T(8,128)(2,1)}, u32[]{:S(2)}, u32[]{:S(2)}) async-start(bf16[48,32,512]{2,0,1:T(8,128)(2,1)} %copy.32), calls=%async_computation.1 | async-start | bytes 3145728 | tf_op jit(solution)/shard_map/all_to_all | solution.py:43
  72.9 171.7 %all-reduce.6.cloned.1.call-start = ((), (), s32[]{:S(2)}) async-start(), calls=%async_computation.2 | async-start | bytes 1572864 | tf_op jit(solution)/shard_map/psum | solution.py:71
  76.8 4.2 collective-permute-start
  78.8 4.4 collective-permute-start.1
  113.8 1.5 copy-start.9
  114.8 305.1 %all-reduce.8.cloned.1.call-start = ((), (), s32[]{:S(2)}) async-start(), calls=%async_computation.3 | async-start | bytes 2097152 | tf_op jit(solution)/shard_map/psum | solution.py:83
  274.9 6.5 %copy-start.1 = (bf16[64,32,512]{2,0,1:T(8,128)(2,1)S(1)}, bf16[64,32,512]{2,0,1:T(8,128)(2,1)}, u32[]{:S(2)}) copy-start(bf16[64,32,512]{2,0,1:T(8,128)(2,1)} %copy-done) | copy-start | bytes 6291460
  275.0 2.7 collective-permute-start.2
  276.4 4.9 collective-permute-start.3
  283.3 311.5 %all-reduce.10.cloned.1.call-start = ((), (), s32[]{:S(2)}) async-start(), calls=%async_computation.4 | async-start | bytes 1572864 | tf_op jit(solution)/shard_map/psum | solution.py:71
  419.9 25.7 %copy-start.4 = (f32[2048,128]{0,1:T(8,128)S(1)}, f32[2048,128]{0,1:T(8,128)}, u32[]{:S(2)}) copy-start(f32[2048,128]{0,1:T(8,128)} %all-reduce.8.cloned.1.call-done) | copy-start | bytes 3145732
  445.6 2.0 copy-start.2
  448.4 2.8 collective-permute-start.4
  449.7 4.9 collective-permute-start.5
  457.9 1.9 copy-start.3
  457.9 1.9 copy-start.5
Sparse Core Ops, SparseCore 0:
  114.9 129.6 all-reduce.5
  283.4 136.5 all-reduce.7
  459.0 135.7 all-reduce.9
where the time goes:
time: 638 us; the launch traced here: 631 us
  waiting for transfers between devices  482 us (76%)
  other arithmetic  74.7 us (12%)
  matrix products  27.9 us (4%)
  starting transfers between devices  20.3 us (3%)
  between operations  14.5 us (2%)
  local copies, waits for them, and re-layouts  11.7 us (2%)
    psum x2, waiting for transfers between devices, forward(): return jnp.where(live_o, lax.psum(part, AXES), 0.0)  263 us
    psum x1, waiting for transfers between devices, backward(): return jnp.where(live_c, lax.psum(part, AXES), 0.0)  136 us
    all_to_all x1, waiting for transfers between devices, per_device(): zc = lax.all_to_all(zc_in[0], AXES, split_axis=1, concat_axis=0, tiled=True)  46 us
    another operation x9, other arithmetic, orth_local(): lower = jnp.linalg.cholesky(square)  37.2 us
    another operation x6, other arithmetic, orth_local(): return jax.scipy.linalg.solve_triangular(lower, matrix.T, lower=True).T  31.4 us
    all_to_all x1, waiting for transfers between devices, per_device(): zo = lax.all_to_all(zo_in[0], AXES, split_axis=1, concat_axis=0, tiled=True)  27.3 us
    dot_general x14, matrix products, dot(): lax.dot_general(left, right, (((contract_left,), (contract_right,)), ((),...  14.9 us
  transfers between devices with their start and end apart: 11, of which 8 were waited for; matrix products, arithmetic and copies ran while one was open for 2% of the time, Pallas kernels for 0%

commit v1 on v0

--- a/solution.py
+++ b/solution.py
@@ -39,7 +39,10 @@
 def per_device(zc_in, zo_in, count_c, count_o, mass, adjacency, ghost_len, omega):
     index = lax.axis_index(AXES)
     devices = lax.axis_size(AXES)
-    zc = lax.all_to_all(zc_in[0], AXES, split_axis=1, concat_axis=0, tiled=True)
+    original = zc_in[0]
+    b_now = jnp.split(original, lax.axis_size(AXES), 1)
+    r_now = jnp.stack(b_now, 0)
+    zc = jnp.concatenate(lax.all_to_all(r_now, AXES, 0, 0), 0)
     zo = lax.all_to_all(zo_in[0], AXES, split_axis=1, concat_axis=0, tiled=True)
     groups = count_c.shape[0]
     live_c = live(count_c, zc.shape[0] // groups)

time: 638 us -> 668 us (1.047)
  local copies, waits for them, and re-layouts: 11.7 us -> 38.9 us
    unnamed x24 -> x57, local copies, waits for them, and re-layouts: 6.85 us -> 35.9 us
  transfers between devices with their start and end apart: 11 -> 11, of which waited for: 8 -> 8; matrix products, arithmetic and copies ran while one was open for 2% -> 1% of each run, Pallas kernels for 0% -> 0%
where the time goes in v1:
time: 668 us; the launch traced here: 662 us
  waiting for transfers between devices  483 us (72%)
  other arithmetic  74.8 us (11%)
  local copies, waits for them, and re-layouts  38.9 us (6%)
  matrix products  29.6 us (4%)
  starting transfers between devices  20.3 us (3%)
  between operations  14.5 us (2%)
    psum x2, waiting for transfers between devices, forward(): return jnp.where(live_o, lax.psum(part, AXES), 0.0)  263 us
    psum x1, waiting for transfers between devices, backward(): return jnp.where(live_c, lax.psum(part, AXES), 0.0)  136 us
    all_to_all x1, waiting for transfers between devices, per_device(): zc = jnp.concatenate(lax.all_to_all(r_now, AXES, 0, 0), 0)  46 us
    another operation x9, other arithmetic, orth_local(): lower = jnp.linalg.cholesky(square)  37.2 us
    unnamed x57, local copies, waits for them, and re-layouts  35.9 us
    another operation x6, other arithmetic, orth_local(): return jax.scipy.linalg.solve_triangular(lower, matrix.T, lower=True).T  31.4 us
    all_to_all x1, waiting for transfers between devices, per_device(): zo = lax.all_to_all(zo_in[0], AXES, split_axis=1, concat_axis=0, tiled=True)  28.8 us
    dot_general x14, matrix products, dot(): lax.dot_general(left, right, (((contract_left,), (contract_right,)), ((),...  15 us
  transfers between devices with their start and end apart: 11, of which 8 were waited for; matrix products, arithmetic and copies ran while one was open for 1% of the time, Pallas kernels for 0%

profile of v1, /device:TPU:0, one launch (start us, length us, event | category | flops | bytes accessed | tf_op | source)
XLA Modules:
  0.0 661.5 jit_solution(4786927188159072241)
XLA Ops:
  40.7 7.3 %all-to-all-start = ((bf16[32,64,512]{2,1,0:T(8,128)(2,1)}), bf16[32,64,512]{2,1,0:T(8,128)(2,1)S(1)}, u32[]{:S(2)}, u32[]{:S(2)}) async-start(bf16[32,64,512]{2,1,0:T(8,128)(2,1)} %constant_dynamic-update-slice_fusion), calls=%async_computation | async-start | bytes 4194304 | tf_op jit(solution)/shard_map/all_to_all | solution.py:45
  50.0 2.0 copy.24
  52.1 46.0 %all-to-all-done = bf16[32,64,512]{2,1,0:T(8,128)(2,1)S(1)} async-done(((bf16[32,64,512]{2,1,0:T(8,128)(2,1)}), bf16[32,64,512]{2,1,0:T(8,128)(2,1)S(1)}, u32[]{:S(2)}, u32[]{:S(2)}) %all-to-all-start) | async-done | bytes 2097184 | tf_op jit(solution)/shard_map/all_to_all | solution.py:45
  98.1 3.5 all-to-all-start.1
  108.3 2.2 collective-permute-done.1
  111.7 28.8 %all-to-all-done.1 = bf16[48,32,512]{2,0,1:T(8,128)(2,1)} async-done(((bf16[48,32,512]{2,0,1:T(8,128)(2,1)}), bf16[48,32,512]{2,0,1:T(8,128)(2,1)}, u32[]{:S(2)}, u32[]{:S(2)}) %all-to-all-start.1) | async-done | bytes 1572896 | tf_op jit(solution)/shard_map/all_to_all | solution.py:46
  140.5 2.0 convolution_bitcast_fusion.1
  144.1 129.1 %all-reduce.6.cloned.1.call-done = f32[1536,128]{0,1:T(8,128)} async-done(((f32[1536,128]{0,1:T(8,128)}), f32[1536,128]{0,1:T(8,128)}) %all-reduce.6.cloned.1.call-update) | async-done | bytes 786448 | tf_op jit(solution)/shard_map/psum | solution.py:74
  273.3 2.2 fusion.25
  275.6 11.7 %cholesky.59 = f32[128,128]{1,0:T(8,128)S(1)} custom-call(f32[128,128]{1,0:T(8,128)S(1)} %fusion.69), custom_call_target="Cholesky" | custom-call | tf_op jit(solution)/shard_map/jit(cholesky)/cholesky | solution.py:35
  288.6 9.8 %custom-call.11 = f32[1,128,128]{1,2,0:T(8,128)S(1)} custom-call(f32[1,128,128]{2,1,0:T(8,128)S(1)} %fusion.61), custom_call_target="InvertDiagBlocksLowerTriangular" | custom-call | tf_op jit(solution)/shard_map/jit(_solve_triangular)/triangular_solve | solution.py:36
  306.4 3.6 collective-permute-done.3
  312.1 136.5 %all-reduce.8.cloned.1.call-done = f32[2048,128]{1,0:T(8,128)} async-done(((f32[2048,128]{1,0:T(8,128)}), f32[2048,128]{1,0:T(8,128)}) %all-reduce.8.cloned.1.call-update) | async-done | bytes 1048592 | tf_op jit(solution)/shard_map/psum | solution.py:86
  448.6 4.0 fusion.13
  452.7 11.7 %cholesky.70 = f32[128,128]{1,0:T(8,128)S(1)} custom-call(f32[128,128]{1,0:T(8,128)S(1)} %fusion.67), custom_call_target="Cholesky" | custom-call | tf_op jit(solution)/shard_map/jit(cholesky)/cholesky | solution.py:35
  465.8 9.8 %custom-call.9 = f32[1,128,128]{1,2,0:T(8,128)S(1)} custom-call(f32[1,128,128]{2,1,0:T(8,128)S(1)} %fusion.62), custom_call_target="InvertDiagBlocksLowerTriangular" | custom-call | tf_op jit(solution)/shard_map/jit(_solve_triangular)/triangular_solve | solution.py:36
  475.6 2.3 reduce-precision_convert_fusion.1
  481.6 3.4 collective-permute-done.5
  486.1 2.0 convolution_bitcast_fusion
  491.3 133.8 %all-reduce.10.cloned.1.call-done = f32[1536,128]{0,1:T(8,128)} async-done(((f32[1536,128]{0,1:T(8,128)}), f32[1536,128]{0,1:T(8,128)}) %all-reduce.10.cloned.1.call-update) | async-done | bytes 786448 | tf_op jit(solution)/shard_map/psum | solution.py:74
  625.1 2.2 fusion.22
  627.4 11.7 %cholesky.81 = f32[128,128]{1,0:T(8,128)S(1)} custom-call(f32[128,128]{1,0:T(8,128)S(1)} %fusion.65), custom_call_target="Cholesky" | custom-call | tf_op jit(solution)/shard_map/jit(cholesky)/cholesky | solution.py:35
  640.5 9.8 %custom-call.12 = f32[1,128,128]{1,2,0:T(8,128)S(1)} custom-call(f32[1,128,128]{2,1,0:T(8,128)S(1)} %fusion.63), custom_call_target="InvertDiagBlocksLowerTriangular" | custom-call | tf_op jit(solution)/shard_map/jit(_solve_triangular)/triangular_solve | solution.py:36
  652.3 2.5 fusion.95
  (125 shorter events, 69.1 us)
Async XLA Ops:
  7.2 23.6 %copy-start.5 = (bf16[1,64,16384]{2,1,0:T(8,128)(2,1)S(1)}, bf16[1,64,16384]{2,1,0:T(8,128)(2,1)}, u32[]{:S(2)}) copy-start(bf16[1,64,16384]{2,1,0:T(8,128)(2,1)} %param.11) | copy-start | bytes 6291460
  40.7 57.4 %all-to-all-start = ((bf16[32,64,512]{2,1,0:T(8,128)(2,1)}), bf16[32,64,512]{2,1,0:T(8,128)(2,1)S(1)}, u32[]{:S(2)}, u32[]{:S(2)}) async-start(bf16[32,64,512]{2,1,0:T(8,128)(2,1)} %constant_dynamic-update-slice_fusion), calls=%async_computation | async-start | bytes 4194304 | tf_op jit(solution)/shard_map/all_to_all | solution.py:45
  50.0 2.0 copy-start.8
  52.0 49.7 %copy-start.10 = (s32[4]{0:T(128)S(1)}, s32[4]{0:T(128)}, u32[]{:S(2)}) copy-start(s32[4]{0:T(128)} %param.13) | copy-start | bytes 52
  52.0 49.7 %copy-start.9 = (s32[4,4]{1,0:T(4,128)S(1)}, s32[4,4]{1,0:T(4,128)}, u32[]{:S(2)}) copy-start(s32[4,4]{1,0:T(4,128)} %param.17) | copy-start | bytes 196
  52.1 50.9 %copy-start.7 = (f32[2048,128]{1,0:T(8,128)S(1)}, f32[2048,128]{1,0:T(8,128)}, u32[]{:S(2)}) copy-start(f32[2048,128]{1,0:T(8,128)} %param.18) | copy-start | bytes 3145732
  98.1 5.2 copy-start
  98.1 42.3 %all-to-all-start.1 = ((bf16[48,32,512]{2,0,1:T(8,128)(2,1)}), bf16[48,32,512]{2,0,1:T(8,128)(2,1)}, u32[]{:S(2)}, u32[]{:S(2)}) async-start(bf16[48,32,512]{2,0,1:T(8,128)(2,1)} %copy.24), calls=%async_computation.1 | async-start | bytes 3145728 | tf_op jit(solution)/shard_map/all_to_all | solution.py:46
  101.6 171.6 %all-reduce.6.cloned.1.call-start = ((), (), s32[]{:S(2)}) async-start(), calls=%async_computation.2 | async-start | bytes 1572864 | tf_op jit(solution)/shard_map/psum | solution.py:74
  104.2 4.2 collective-permute-start
  106.1 4.4 collective-permute-start.1
  142.5 1.5 copy-start.11
  143.5 305.1 %all-reduce.8.cloned.1.call-start = ((), (), s32[]{:S(2)}) async-start(), calls=%async_computation.3 | async-start | bytes 2097152 | tf_op jit(solution)/shard_map/psum | solution.py:86
  303.5 6.5 copy-start.1
  303.6 2.7 collective-permute-start.2
  305.1 4.9 collective-permute-start.3
  311.9 313.2 %all-reduce.10.cloned.1.call-start = ((), (), s32[]{:S(2)}) async-start(), calls=%async_computation.4 | async-start | bytes 1572864 | tf_op jit(solution)/shard_map/psum | solution.py:74
  448.6 27.0 %copy-start.4 = (f32[2048,128]{1,0:T(8,128)S(1)}, f32[2048,128]{1,0:T(8,128)}, u32[]{:S(2)}) copy-start(f32[2048,128]{1,0:T(8,128)} %all-reduce.8.cloned.1.call-done) | copy-start | bytes 3145732
  475.6 2.3 copy-start.2
  478.7 2.8 collective-permute-start.4
  480.1 4.9 collective-permute-start.5
  488.2 1.9 copy-start.3
  488.2 1.9 copy-start.6
Sparse Core Ops, SparseCore 0:
  143.6 129.5 all-reduce.5
  312.0 136.5 all-reduce.7
  489.3 135.7 all-reduce.9
